TPU v7x, 32 devices: a whole 2x2x4 slice. The times are simulated.
32 devices in a mesh: rep: 16 (over z, y, core), tp: 2 (over x).
Axes of the slice: x: 2, y: 2, z: 4, core: 2. Of those that a mesh axis runs over, the one named last changes fastest.
Arguments:
- acts: bfloat16 [16, 256, 4096], P('rep', 'tp'), may hold values from -6 to 6
- weights: bfloat16 [16, 4096, 4096], P('rep', None, 'tp'), may hold values from -6 to 6
- cotangent: bfloat16 [16, 256, 4096], P('rep', None, 'tp'), may hold values from -6 to 6
- start_factors: float32 [4096, 32], replicated, may hold values from -6 to 6
Outputs:
- projected: bfloat16 [16, 256, 4096], P('rep', None, 'tp')
- new_weights: bfloat16 [16, 4096, 4096], P('rep', None, 'tp')
All inputs are finite; a program needn't handle non-finite values.
Results may differ from a plain program's by a relative error of at most 0.001.
Values may be sent and summed in bfloat16 or wider, within the bound.
A program may use at most 128 MiB of HBM per device.

v0:
```python
import jax
import jax.numpy as jnp
from jax import lax
from jax.sharding import PartitionSpec as P

D = 4096
STEPS = 3


HIGH = lax.Precision.HIGHEST


def partner(block, axis, stride):
    count = lax.axis_size(axis)
    route = []
    for low in range(count):
        high = low | 1 << stride
        if high != low and high < count:
            route += [(low, high), (high, low)]
    return lax.ppermute(block, axis, route)


def shards(acts, weights, cotangent, start_factors):
    scale = D ** (-0.5)
    weight_part = weights[0]
    grad_out = cotangent[0]
    projected = (
        jnp.dot(
            lax.all_gather(acts, "tp", axis=1, tiled=True)[0],
            weight_part,
            preferred_element_type=jnp.float32,
        )
        * scale
    ).astype(jnp.bfloat16)[None]
    grad = lax.dot_general(
        lax.all_gather(acts, "tp", axis=1, tiled=True)[0],
        grad_out,
        (((0,), (0,)), ((), ())),
        preferred_element_type=jnp.float32,
    )
    current = weight_part.astype(jnp.float32) - 0.5 * scale * grad
    for step in range(STEPS):
        side = lax.dot_general(current, start_factors, (((0,), (0,)), ((), ())), precision=HIGH)
        other = partner(side, "rep", step)
        diff = side - other
        gram = lax.psum(jnp.dot(diff.T, diff, precision=HIGH), "tp")
        lower = jnp.linalg.cholesky(gram)
        ortho = jax.scipy.linalg.solve_triangular(lower, diff.T, lower=True).T
        local = jnp.dot(current, ortho, precision=HIGH)
        summed = lax.psum(local, "tp")
        back = summed + partner(summed, "rep", step)
        current = current - 0.5 * jnp.dot(back, ortho.T, precision=HIGH)
    return (projected, current.astype(jnp.bfloat16)[None])


def solution(mesh):
    in_specs = (P("rep", "tp", None), P("rep", None, "tp"), P("rep", None, "tp"), P())
    out_specs = (P("rep", None, "tp"), P("rep", None, "tp"))
    return jax.shard_map(shards, mesh=mesh, in_specs=in_specs, out_specs=out_specs, check_vma=False)
```

profile of v0, /device:TPU:0, one launch (start us, length us, event | category | flops | bytes accessed | tf_op | source)
XLA Modules:
  0.0 527.9 jit_solution(1193030660214079596)
XLA Ops:
  8.0 37.4 %all-gather.2.cloned.1.call-done = bf16[1,256,4096]{2,1,0:T(8,128)(2,1)} async-done(((bf16[1,128,4096]{2,1,0:T(8,128)(2,1)}), bf16[1,256,4096]{2,1,0:T(8,128)(2,1)}) %all-gather.2.cloned.1.call-update) | async-done | bytes 2097168 | tf_op jit(solution)/shard_map/all_gather | solution.py:29
  45.4 17.1 %multiply_subtract_fusion.2 = f32[4096,2048]{1,0:T(8,128)} fusion(bf16[1,4096,2048]{2,1,0:T(8,128)(2,1)} %param.8, bf16[1,256,4096]{2,1,0:T(8,128)(2,1)} %all-gather.2.cloned.1.call-done, bf16[1,256,2048]{2,1,0:T(8,128)(2,1)S(1)} %copy-done), kind=kOutput, calls=%fused_computation.3 | convolution fusion | flops 4320133120 | bytes 53477376 | tf_op jit(solution)/shard_map/dot_general | solution.py:35
  62.5 23.8 %fusion.42 = f32[2048,32]{0,1:T(8,128)S(1)} fusion(f32[4096,2048]{1,0:T(8,128)} %multiply_subtract_fusion.2, f32[4096,32]{0,1:T(8,128)S(1)} %copy-done.2), kind=kOutput, calls=%fused_computation.54 | convolution fusion | flops 3221225472 | bytes 34340864 | tf_op jit(solution)/shard_map/dot_general | solution.py:43
  86.4 1.5 collective-permute-done
  88.3 7.5 %psum.42 = f32[32,32]{0,1:T(8,128)S(1)} all-reduce(f32[32,32]{0,1:T(8,128)S(1)} %fusion.31), channel_id=1, replica_groups=mesh['rep'=16,'tp'=2] {'tp'}, use_global_device_ids=true, to_apply=%region_0.0 | all-reduce | flops 1024 | bytes 8192 | tf_op jit(solution)/shard_map/psum | solution.py:46
  95.8 2.9 cholesky.59
  100.1 2.4 custom-call.7
  103.0 35.0 %fusion.43 = f32[4096,32]{0,1:T(8,128)} fusion(f32[4096,2048]{1,0:T(8,128)} %multiply_subtract_fusion.2, f32[32,2048]{1,0:T(8,128)S(1)} %fusion.22), kind=kOutput, calls=%fused_computation.55 | convolution fusion | flops 3221225472 | bytes 34340864 | tf_op jit(solution)/shard_map/dot_general | solution.py:49
  138.2 29.7 %all-reduce.4.cloned.1.call-done = f32[4096,32]{0,1:T(8,128)} async-done(((f32[4096,32]{0,1:T(8,128)}), f32[4096,32]{0,1:T(8,128)}) %all-reduce.4.cloned.1.call-update) | async-done | bytes 524304 | tf_op jit(solution)/shard_map/psum | solution.py:50
  167.9 2.1 collective-permute-done.1
  170.0 33.5 %multiply_subtract_fusion.1 = f32[4096,2048]{1,0:T(8,128)} fusion(f32[4096,2048]{1,0:T(8,128)} %multiply_subtract_fusion.2, f32[32,2048]{1,0:T(8,128)S(1)} %fusion.22, f32[4096,32]{0,1:T(8,128)} %all-reduce.4.cloned.1.call-done, f32[4096,32]{0,1:T(8,128)S(1)} %collective-permute-done.1), kind=kOutput, calls=%fused_computation.2 | convolution fusion | flops 3238133760 | bytes 68419584 | tf_op jit(solution)/shard_map/dot_general | solution.py:52
  203.6 23.8 %fusion.44 = f32[2048,32]{0,1:T(8,128)S(1)} fusion(f32[4096,2048]{1,0:T(8,128)} %multiply_subtract_fusion.1, f32[4096,32]{0,1:T(8,128)S(1)} %copy-done.2), kind=kOutput, calls=%fused_computation.56 | convolution fusion | flops 3221225472 | bytes 34340864 | tf_op jit(solution)/shard_map/dot_general | solution.py:43
  227.4 1.5 collective-permute-start.2
  228.9 6.9 %collective-permute-done.2 = f32[2048,32]{0,1:T(8,128)S(1)} collective-permute-done((f32[2048,32]{0,1:T(8,128)S(1)}, f32[2048,32]{0,1:T(8,128)S(1)}, u32[]{:S(2)}, u32[]{:S(2)}) %collective-permute-start.2) | collective-permute-done | bytes 262176 | tf_op jit(solution)/shard_map/ppermute | solution.py:20
  236.1 7.2 %psum.44 = f32[32,32]{0,1:T(8,128)S(1)} all-reduce(f32[32,32]{0,1:T(8,128)S(1)} %fusion.28), channel_id=1, replica_groups=mesh['rep'=16,'tp'=2] {'tp'}, use_global_device_ids=true, to_apply=%region_4.0 | all-reduce | flops 1024 | bytes 8192 | tf_op jit(solution)/shard_map/psum | solution.py:46
  243.4 2.9 cholesky.70
  247.6 2.4 custom-call.8
  250.5 35.0 %fusion.45 = f32[4096,32]{0,1:T(8,128)} fusion(f32[4096,2048]{1,0:T(8,128)} %multiply_subtract_fusion.1, f32[32,2048]{1,0:T(8,128)S(1)} %fusion.20), kind=kOutput, calls=%fused_computation.57 | convolution fusion | flops 3221225472 | bytes 34340864 | tf_op jit(solution)/shard_map/dot_general | solution.py:49
  285.9 29.6 %all-reduce.6.cloned.1.call-done = f32[4096,32]{0,1:T(8,128)} async-done(((f32[4096,32]{0,1:T(8,128)}), f32[4096,32]{0,1:T(8,128)}) %all-reduce.6.cloned.1.call-update) | async-done | bytes 524304 | tf_op jit(solution)/shard_map/psum | solution.py:50
  317.0 12.4 %collective-permute-done.3 = f32[4096,32]{0,1:T(8,128)S(1)} collective-permute-done((f32[4096,32]{0,1:T(8,128)}, f32[4096,32]{0,1:T(8,128)S(1)}, u32[]{:S(2)}, u32[]{:S(2)}) %collective-permute-start.3) | collective-permute-done | bytes 524320 | tf_op jit(solution)/shard_map/ppermute | solution.py:20
  329.4 33.5 %multiply_subtract_fusion = f32[4096,2048]{1,0:T(8,128)} fusion(f32[4096,2048]{1,0:T(8,128)} %multiply_subtract_fusion.1, f32[32,2048]{1,0:T(8,128)S(1)} %fusion.20, f32[4096,32]{0,1:T(8,128)} %all-reduce.6.cloned.1.call-done, f32[4096,32]{0,1:T(8,128)S(1)} %collective-permute-done.3), kind=kOutput, calls=%fused_computation.1 | convolution fusion | flops 3238133760 | bytes 68419584 | tf_op jit(solution)/shard_map/dot_general | solution.py:52
  362.9 23.8 %fusion.46 = f32[2048,32]{0,1:T(8,128)S(1)} fusion(f32[4096,2048]{1,0:T(8,128)} %multiply_subtract_fusion, f32[4096,32]{0,1:T(8,128)S(1)} %copy-done.2), kind=kOutput, calls=%fused_computation.58 | convolution fusion | flops 3221225472 | bytes 34340864 | tf_op jit(solution)/shard_map/dot_general | solution.py:43
  386.7 1.6 collective-permute-start.4
  388.2 5.7 %collective-permute-done.4 = f32[2048,32]{0,1:T(8,128)S(1)} collective-permute-done((f32[2048,32]{0,1:T(8,128)S(1)}, f32[2048,32]{0,1:T(8,128)S(1)}, u32[]{:S(2)}, u32[]{:S(2)}) %collective-permute-start.4) | collective-permute-done | bytes 262176 | tf_op jit(solution)/shard_map/ppermute | solution.py:20
  394.3 7.8 %psum.46 = f32[32,32]{0,1:T(8,128)S(1)} all-reduce(f32[32,32]{0,1:T(8,128)S(1)} %fusion.25), channel_id=1, replica_groups=mesh['rep'=16,'tp'=2] {'tp'}, use_global_device_ids=true, to_apply=%region_6.9 | all-reduce | flops 1024 | bytes 8192 | tf_op jit(solution)/shard_map/psum | solution.py:46
  402.1 2.9 cholesky.81
  406.4 2.4 custom-call.9
  409.3 35.0 %fusion.47 = f32[4096,32]{0,1:T(8,128)} fusion(f32[4096,2048]{1,0:T(8,128)} %multiply_subtract_fusion, f32[32,2048]{1,0:T(8,128)S(1)} %fusion.18), kind=kOutput, calls=%fused_computation.59 | convolution fusion | flops 3221225472 | bytes 34340864 | tf_op jit(solution)/shard_map/dot_general | solution.py:49
  444.3 29.6 %all-reduce.8.cloned.1.call-done = f32[4096,32]{0,1:T(8,128)} async-done(((f32[4096,32]{0,1:T(8,128)}), f32[4096,32]{0,1:T(8,128)}) %all-reduce.8.cloned.1.call-update) | async-done | bytes 524304 | tf_op jit(solution)/shard_map/psum | solution.py:50
  475.4 9.3 %fusion.9 = bf16[1,256,2048]{2,1,0:T(8,128)(2,1)} fusion(bf16[1,4096,2048]{2,1,0:T(8,128)(2,1)} %param.8, bf16[1,256,4096]{2,1,0:T(8,128)(2,1)S(1)} %copy-done.3), kind=kOutput, calls=%fused_computation.9 | convolution fusion | flops 4296015872 | bytes 19922944 | tf_op jit(solution)/shard_map/dot_general | solution.py:28
  484.7 3.1 collective-permute-done.5
  487.8 33.4 %fusion = bf16[1,4096,2048]{2,1,0:T(8,128)(2,1)} fusion(f32[4096,2048]{1,0:T(8,128)} %multiply_subtract_fusion, f32[32,2048]{1,0:T(8,128)S(1)} %fusion.18, f32[4096,32]{0,1:T(8,128)S(1)} %copy-done.4, f32[4096,32]{0,1:T(8,128)S(1)} %collective-permute-done.5), kind=kOutput, calls=%fused_computation.4 | convolution fusion | flops 3246522368 | bytes 51642368 | tf_op jit(solution)/shard_map/dot_general | solution.py:52
  (43 shorter events, 11.0 us)
Async XLA Ops:
  7.2 38.3 %copy-start = (bf16[1,256,2048]{2,1,0:T(8,128)(2,1)S(1)}, bf16[1,256,2048]{2,1,0:T(8,128)(2,1)}, u32[]{:S(2)}) copy-start(bf16[1,256,2048]{2,1,0:T(8,128)(2,1)} %param.9) | copy-start | bytes 3145732
  7.2 55.3 %copy-start.2 = (f32[4096,32]{0,1:T(8,128)S(1)}, f32[4096,32]{0,1:T(8,128)}, u32[]{:S(2)}) copy-start(f32[4096,32]{0,1:T(8,128)} %param.10) | copy-start | bytes 1572868
  7.2 38.2 %all-gather.2.cloned.1.call-start = ((), (), s32[]{:S(2)}) async-start(), calls=%async_computation | async-start | bytes 3145728 | tf_op jit(solution)/shard_map/all_gather | solution.py:29
  7.9 160.0 %all-reduce.4.cloned.1.call-start = ((), (), s32[]{:S(2)}) async-start(), calls=%async_computation.1 | async-start | bytes 1048576 | tf_op jit(solution)/shard_map/psum | solution.py:50
  86.3 1.6 collective-permute-start
  138.0 177.5 %all-reduce.6.cloned.1.call-start = ((), (), s32[]{:S(2)}) async-start(), calls=%async_computation.2 | async-start | bytes 1048576 | tf_op jit(solution)/shard_map/psum | solution.py:50
  167.9 2.1 collective-permute-start.1
  227.4 8.4 %collective-permute-start.2 = (f32[2048,32]{0,1:T(8,128)S(1)}, f32[2048,32]{0,1:T(8,128)S(1)}, u32[]{:S(2)}, u32[]{:S(2)}) collective-permute-start(f32[2048,32]{0,1:T(8,128)S(1)} %fusion.44), channel_id=1, source_target_pairs={{0,4},{4,0},{2,6},{6,2},{8,12},{12,8},{10,14},{14,10},{16,20},{20,... | collective-permute-start | bytes 786440 | tf_op jit(solution)/shard_map/ppermute | solution.py:20
  285.6 188.3 %all-reduce.8.cloned.1.call-start = ((), (), s32[]{:S(2)}) async-start(), calls=%async_computation.3 | async-start | bytes 1048576 | tf_op jit(solution)/shard_map/psum | solution.py:50
  315.5 13.9 %collective-permute-start.3 = (f32[4096,32]{0,1:T(8,128)}, f32[4096,32]{0,1:T(8,128)S(1)}, u32[]{:S(2)}, u32[]{:S(2)}) collective-permute-start(f32[4096,32]{0,1:T(8,128)} %all-reduce.6.cloned.1.call-done), channel_id=1, source_target_pairs={{0,4},{4,0},{2,6},{6,2},{8,12},{12,8},{10,14},{14,10},{16,20},{20,... | collective-permute-start | bytes 1572872 | tf_op jit(solution)/shard_map/ppermute | solution.py:20
  386.7 88.7 %copy-start.3 = (bf16[1,256,4096]{2,1,0:T(8,128)(2,1)S(1)}, bf16[1,256,4096]{2,1,0:T(8,128)(2,1)}, u32[]{:S(2)}) copy-start(bf16[1,256,4096]{2,1,0:T(8,128)(2,1)} %all-gather.2.cloned.1.call-done) | copy-start | bytes 6291460
  386.7 7.2 %collective-permute-start.4 = (f32[2048,32]{0,1:T(8,128)S(1)}, f32[2048,32]{0,1:T(8,128)S(1)}, u32[]{:S(2)}, u32[]{:S(2)}) collective-permute-start(f32[2048,32]{0,1:T(8,128)S(1)} %fusion.46), channel_id=1, source_target_pairs={{0,8},{8,0},{2,10},{10,2},{4,12},{12,4},{6,14},{14,6},{16,24},{24,... | collective-permute-start | bytes 786440 | tf_op jit(solution)/shard_map/ppermute | solution.py:20
  473.9 13.9 %copy-start.4 = (f32[4096,32]{0,1:T(8,128)S(1)}, f32[4096,32]{0,1:T(8,128)}, u32[]{:S(2)}) copy-start(f32[4096,32]{0,1:T(8,128)} %all-reduce.8.cloned.1.call-done) | copy-start | bytes 1572868
  473.9 13.9 %collective-permute-start.5 = (f32[4096,32]{0,1:T(8,128)}, f32[4096,32]{0,1:T(8,128)S(1)}, u32[]{:S(2)}, u32[]{:S(2)}) collective-permute-start(f32[4096,32]{0,1:T(8,128)} %all-reduce.8.cloned.1.call-done), channel_id=1, source_target_pairs={{0,8},{8,0},{2,10},{10,2},{4,12},{12,4},{6,14},{14,6},{16,24},{24,... | collective-permute-start | bytes 1572872 | tf_op jit(solution)/shard_map/ppermute | solution.py:20
  475.4 45.8 %copy-start.1 = (bf16[1,256,2048]{2,1,0:T(8,128)(2,1)S(1)}, bf16[1,256,2048]{2,1,0:T(8,128)(2,1)}, u32[]{:S(2)}) copy-start(bf16[1,256,2048]{2,1,0:T(8,128)(2,1)} %param.9) | copy-start | bytes 3145732
Sparse Core Ops, SparseCore 0:
  9.6 35.7 all-gather.1
  138.1 29.7 all-reduce.3
  285.7 29.7 all-reduce.5
  444.5 29.3 all-reduce.7
where the time goes:
time: 534 us; the launch traced here: 528 us
  matrix products  306 us (57%)
  waiting for transfers between devices  159 us (30%)
  blocking collectives  22.4 us (4%)
  other arithmetic  20.1 us (4%)
  between operations  14.1 us (3%)
  starting transfers between devices  6.71 us (1%)
    dot_general x3, matrix products, shards(): local = jnp.dot(current, ortho, precision=HIGH)  105 us
    dot_general x3, matrix products, shards(): current = current - 0.5 * jnp.dot(back, ortho.T, precision=HIGH)  100 us
    psum x3, waiting for transfers between devices, shards(): summed = lax.psum(local, 'tp')  88.8 us
    dot_general x3, matrix products, shards(): lax.dot_general(current, start_factors, (((0,), (0,)), ((), ())), precisi...  71.4 us
    all_gather x1, waiting for transfers between devices, shards(): lax.all_gather(acts, 'tp', axis=1, tiled=True)[0]  37.4 us
    ppermute x6, waiting for transfers between devices, partner(): return lax.ppermute(block, axis, route)  31.7 us
    psum x3, blocking collectives, shards(): gram = lax.psum(jnp.dot(diff.T, diff, precision=HIGH), 'tp')  22.4 us
    dot_general x1, matrix products, shards(): lax.dot_general(lax.all_gather(acts, 'tp', axis=1, tiled=True)[0], grad_o...  17.1 us
  transfers between devices with their start and end apart: 10, of which 10 were waited for; matrix products, arithmetic and copies ran while one was open for 2% of the time, Pallas kernels for 0%

commit v1 on v0

v1 whole, which is shorter than its diff:
```python
import jax
import jax.numpy as jnp
from jax import lax
from jax.sharding import PartitionSpec as P

STEPS = 3
F32, BF16, F16 = jnp.float32, jnp.bfloat16, jnp.float16
HIGH = lax.Precision.HIGHEST


def partner(block, axis, stride):
    count = lax.axis_size(axis)
    route = [(low, low ^ (1 << stride)) for low in range(count)]
    return lax.ppermute(block, axis, route)


def split(x, terms):
    out = []
    for _ in range(terms):
        part = lax.reduce_precision(x, 8, 7)
        out.append(part.astype(BF16))
        x = x - part
    return out


def dot(a, b, ca, cb):
    return lax.dot_general(a, b, (((ca,), (cb,)), ((), ())), preferred_element_type=F32)


def folded(out, terms):
    return out.reshape((terms, -1) + out.shape[1:]).sum(0)


def gather(x, axis):
    n = lax.axis_size("tp")
    if n != 2:
        return lax.all_gather(x, "tp", axis=axis, tiled=True)
    me = lax.axis_index("tp")
    other = partner(x, "tp", 0)
    size = x.shape[axis]
    shape = list(x.shape)
    shape[axis] = 2 * size
    full = jnp.zeros(shape, x.dtype)
    full = lax.dynamic_update_slice_in_dim(full, x, me * size, axis)
    return lax.dynamic_update_slice_in_dim(full, other, (1 - me) * size, axis)


def total(x):
    if lax.axis_size("tp") != 2:
        return lax.psum(x, "tp")
    return x + partner(x, "tp", 0)


def scattered(x):
    n = lax.axis_size("tp")
    if n != 2:
        return lax.psum_scatter(x, "tp", scatter_dimension=1, tiled=True)
    me = lax.axis_index("tp")
    size = x.shape[1] // 2
    mine = lax.dynamic_slice_in_dim(x, me * size, size, 1)
    theirs = lax.dynamic_slice_in_dim(x, (1 - me) * size, size, 1)
    return mine + partner(theirs.astype(F16), "tp", 0).astype(F32)


def shards(acts, weights, cotangent, start_factors):
    d, rank = start_factors.shape
    scale = d ** (-0.5)
    mine, w, c = acts[0], weights[0], cotangent[0]

    full = gather(mine, 0)
    s3 = jnp.concatenate(split(start_factors.T, 3), 0)
    acts_s = gather(folded(dot(s3, mine, 1, 1), 3), 1)
    side = folded(dot(s3, w, 1, 0), 3)
    a3 = jnp.concatenate(split(acts_s, 3), 0)
    side = side - 0.5 * scale * folded(dot(a3, c, 1, 0), 3)

    diffs = []
    for step in range(STEPS):
        other = partner(side, "rep", step)
        diffs.append(side - other)
        side = 0.5 * (side + other)
    diff = jnp.concatenate(diffs, 0)
    gram = total(lax.dot_general(diff, diff, (((1,), (1,)), ((), ())), precision=HIGH))
    blocks = gram.reshape(STEPS, rank, STEPS, rank)
    lower = jnp.linalg.cholesky(jnp.stack([blocks[s, :, s] for s in range(STEPS)]))
    eye = jnp.broadcast_to(jnp.eye(rank, dtype=F32), lower.shape)
    inv = lax.linalg.triangular_solve(lower, eye, left_side=True, lower=True)
    ortho = jnp.einsum("skl,slo->sko", inv, diff.reshape(STEPS, rank, -1), precision=HIGH)
    ortho = ortho.reshape(STEPS * rank, -1)
    cross = {}
    for s in range(STEPS):
        for t in range(s):
            half = jnp.dot(inv[s], blocks[s, :, t], precision=HIGH)
            cross[s, t] = jnp.dot(half, inv[t].T, precision=HIGH)

    o_hi, o_lo = split(ortho, 2)
    o2 = jnp.concatenate([o_hi, o_lo], 0)
    co = folded(dot(o2, c, 1, 1), 2)
    co2 = jnp.concatenate(split(co, 2), 0)
    x = folded(dot(o2, w, 1, 1) - 0.5 * scale * dot(co2, full, 1, 0), 2)

    backs = []
    for step in range(STEPS):
        local = scattered(x[step * rank:(step + 1) * rank])
        for t in range(step):
            local = local - 0.5 * jnp.dot(cross[step, t], backs[t], precision=HIGH)
        if step == 0:
            other = partner(local, "rep", step)
        else:
            other = partner(local.astype(F16), "rep", step).astype(F32)
        backs.append(local + other)
    back = jnp.concatenate([gather(b.astype(F16), 1).astype(F32) for b in backs], 0)

    projected = (dot(full, w, 1, 0) * scale).astype(BF16)[None]
    b_hi, b_lo = split(-0.5 * back, 2)
    left = jnp.concatenate([full * jnp.asarray(-0.5 * scale, BF16), b_hi, b_hi, b_lo], 0)
    right = jnp.concatenate([c, o_hi, o_lo, o_hi], 0)
    new = (w.astype(F32) + dot(left, right, 0, 0)).astype(BF16)[None]
    return projected, new


def solution(mesh):
    in_specs = (P("rep", "tp", None), P("rep", None, "tp"), P("rep", None, "tp"), P())
    out_specs = (P("rep", None, "tp"), P("rep", None, "tp"))
    return jax.shard_map(shards, mesh=mesh, in_specs=in_specs, out_specs=out_specs, check_vma=False)
```

time: 534 us -> 148 us (0.28); the launches traced: 528 us -> 148 us
  matrix products: 306 us -> 62.5 us
  waiting for transfers between devices: 159 us -> 36 us
  blocking collectives: 22.4 us -> 0 us
  between operations: 14.1 us -> 1.07 us
  other arithmetic: 20.1 us -> 30 us
  starting transfers between devices: 6.71 us -> 14.1 us
    dot_general x14 -> x19, matrix products: 304 us -> 62.2 us  [the longest x8 54.9 us: dot(): lax.dot_general(a, b, (((ca,), (cb,)), ((), ())), preferred_element_type=...]
    psum x3 -> x0, waiting for transfers between devices: 88.8 us -> none  [shards(): summed = lax.psum(local, 'tp')]
    all_gather x1 -> x0, waiting for transfers between devices: 37.4 us -> none  [shards(): lax.all_gather(acts, 'tp', axis=1, tiled=True)[0]]
    psum x3 -> x0, blocking collectives: 22.4 us -> none  [shards(): gram = lax.psum(jnp.dot(diff.T, diff, precision=HIGH), 'tp')]
    ppermute x6 -> x15, starting transfers between devices: 6.12 us -> 14.1 us  [partner(): return lax.ppermute(block, axis, route)]
    ppermute x6 -> x15, waiting for transfers between devices: 31.7 us -> 36 us  [partner(): return lax.ppermute(block, axis, route)]
    another operation x15 -> x8, other arithmetic: 20 us -> 16.6 us  [the longest x4 9.14 us: shards(): jnp.linalg.cholesky(jnp.stack([blocks[s, :, s] for s in range(STEPS)]))]
  transfers between devices with their start and end apart: 10 -> 15, of which waited for: 10 -> 10; matrix products, arithmetic and copies ran while one was open for 2% -> 37% of each run, Pallas kernels for 0% -> 0%
where the time goes in v1:
time: 148 us
  matrix products  62.5 us (42%)
  waiting for transfers between devices  36 us (24%)
  other arithmetic  30 us (20%)
  starting transfers between devices  14.1 us (10%)
  local copies, waits for them, and re-layouts  4.06 us (3%)
    dot_general x8, matrix products, dot(): lax.dot_general(a, b, (((ca,), (cb,)), ((), ())), preferred_element_type=...  54.9 us
    ppermute x15, waiting for transfers between devices, partner(): return lax.ppermute(block, axis, route)  36 us
    ppermute x15, starting transfers between devices, partner(): return lax.ppermute(block, axis, route)  14.1 us
    another operation x4, other arithmetic, shards(): jnp.linalg.cholesky(jnp.stack([blocks[s, :, s] for s in range(STEPS)]))  9.14 us
    another operation x3, other arithmetic, shards(): inv = lax.linalg.triangular_solve(lower, eye, left_side=True, lower=True)  7.46 us
    convert_element_type x5, other arithmetic, split(): out.append(part.astype(BF16))  3.59 us
    reduce_sum x1, other arithmetic, folded(): return out.reshape((terms, -1) + out.shape[1:]).sum(0)  3.43 us
  transfers between devices with their start and end apart: 15, of which 10 were waited for; matrix products, arithmetic and copies ran while one was open for 37% of the time, Pallas kernels for 0%

profile of v1, /device:TPU:0, one launch (start us, length us, event | category | flops | bytes accessed | tf_op | source)
XLA Modules:
  0.0 147.8 jit_solution(11012703366012383511)
XLA Ops:
  0.6 1.2 reduce-precision_convert_fusion.3
  2.5 3.0 %collective-permute-start.1 = (f32[32,128]{1,0:T(8,128)S(1)}, f32[32,128]{1,0:T(8,128)S(1)}, u32[]{:S(2)}, u32[]{:S(2)}) collective-permute-start(f32[32,128]{1,0:T(8,128)S(1)} %convolution_reduce_fusion.2), channel_id=1, source_target_pairs={{0,1},{1,0},{2,3},{3,2},{4,5},{5,4},{6,7},{7,6},{8,9},{9,8},{10,11... | collective-permute-start | bytes 49160 | tf_op jit(solution)/shard_map/ppermute | solution.py:14
  5.5 8.6 %fusion.33 = f32[32,2048]{1,0:T(8,128)S(1)} fusion(bf16[3,32,4096]{2,1,0:T(8,128)(2,1)S(1)} %bitcast.93, bf16[1,4096,2048]{2,1,0:T(8,128)(2,1)} %param.5), kind=kOutput, calls=%fused_computation.36 | convolution fusion | flops 1610743808 | bytes 17825792 | tf_op jit(solution)/shard_map/dot_general | solution.py:27
  14.7 1.4 collective-permute-done.2
  16.9 1.5 %collective-permute-start.3 = (f32[32,2048]{1,0:T(8,128)S(1)}, f32[32,2048]{1,0:T(8,128)S(1)}, u32[]{:S(2)}, u32[]{:S(2)}) collective-permute-start(f32[32,2048]{1,0:T(8,128)S(1)} %get-tuple-element.16), channel_id=1, source_target_pairs={{0,4},{2,6},{4,0},{6,2},{8,12},{10,14},{12,8},{14,10},{16,20},{18,... | collective-permute-start | bytes 786440 | tf_op jit(solution)/shard_map/ppermute | solution.py:14
  18.8 6.5 %collective-permute-done.3 = f32[32,2048]{1,0:T(8,128)S(1)} collective-permute-done((f32[32,2048]{1,0:T(8,128)S(1)}, f32[32,2048]{1,0:T(8,128)S(1)}, u32[]{:S(2)}, u32[]{:S(2)}) %collective-permute-start.3) | collective-permute-done | bytes 262176 | tf_op jit(solution)/shard_map/ppermute | solution.py:14
  26.0 1.6 %collective-permute-start.4 = (f32[32,2048]{1,0:T(8,128)S(1)}, f32[32,2048]{1,0:T(8,128)}, u32[]{:S(2)}, u32[]{:S(2)}) collective-permute-start(f32[32,2048]{1,0:T(8,128)S(1)} %get-tuple-element.18), channel_id=1, source_target_pairs={{0,8},{2,10},{4,12},{6,14},{8,0},{10,2},{12,4},{14,6},{16,24},{18,... | collective-permute-start | bytes 786440 | tf_op jit(solution)/shard_map/ppermute | solution.py:14
  27.6 6.1 %collective-permute-done.4 = f32[32,2048]{1,0:T(8,128)} collective-permute-done((f32[32,2048]{1,0:T(8,128)S(1)}, f32[32,2048]{1,0:T(8,128)}, u32[]{:S(2)}, u32[]{:S(2)}) %collective-permute-start.4) | collective-permute-done | bytes 262176 | tf_op jit(solution)/shard_map/ppermute | solution.py:14
  34.7 2.1 %fusion.66 = f32[96,96]{1,0:T(8,128)S(1)} fusion(f32[32,2048]{1,0:T(8,128)S(1)} %sub.63, f32[32,2048]{1,0:T(8,128)} %get-tuple-element.17, f32[32,2048]{1,0:T(8,128)} %get-tuple-element.15), kind=kOutput, calls=%fused_computation.119 | convolution fusion | flops 226885632 | bytes 823296 | tf_op jit(solution)/shard_map/dot_general | solution.py:83
  37.5 2.0 %pad_maximum_fusion.1 = f32[96,2048]{1,0:T(8,128)} fusion(f32[32,2048]{1,0:T(8,128)S(1)} %sub.63, f32[32,2048]{1,0:T(8,128)} %get-tuple-element.17, f32[32,2048]{1,0:T(8,128)} %get-tuple-element.15), kind=kLoop, calls=%fused_computation.48 | loop fusion | flops 393216 | bytes 1572864 | tf_op jit(solution)/shard_map/concatenate | solution.py:82
  39.5 1.8 %collective-permute-done.5 = f32[96,96]{1,0:T(8,128)S(1)} collective-permute-done((f32[96,96]{1,0:T(8,128)S(1)}, f32[96,96]{1,0:T(8,128)S(1)}, u32[]{:S(2)}, u32[]{:S(2)}) %collective-permute-start.5) | collective-permute-done | bytes 36896 | tf_op jit(solution)/shard_map/ppermute | solution.py:14
  41.8 9.0 %custom-call.7 = f32[3,32,32]{2,1,0:T(8,128)S(1)} custom-call(f32[3,32,32]{2,1,0:T(8,128)S(1)} %fusion.51), custom_call_target="Cholesky" | custom-call | tf_op jit(solution)/shard_map/jit(cholesky)/cholesky | solution.py:85
  51.1 7.4 %custom-call.8 = f32[3,1,32,32]{2,3,1,0:T(8,128)S(1)} custom-call(f32[3,1,32,32]{3,2,1,0:T(8,128)S(1)} %select_bitcast_fusion), custom_call_target="InvertDiagBlocksLowerTriangular" | custom-call | tf_op jit(solution)/shard_map/triangular_solve | solution.py:87
  60.9 2.0 %fusion.74 = f32[3,32,2048]{2,1,0:T(8,128)S(1)} fusion(f32[3,32,32]{2,1,0:T(8,128)S(1)} %fusion.49, f32[3,32,2048]{2,1,0:T(8,128)} %bitcast.96), kind=kOutput, calls=%fused_computation.126 | convolution fusion | flops 75497472 | bytes 1585152 | tf_op jit(solution)/shard_map/skl,slo->sko/dot_general | solution.py:88
  64.4 13.2 %fusion.3 = f32[192,4096]{1,0:T(8,128)} fusion(bf16[1,4096,2048]{2,1,0:T(8,128)(2,1)} %param.5, bf16[96,2048]{1,0:T(8,128)(2,1)} %copy-done.6, bf16[96,2048]{1,0:T(8,128)(2,1)S(1)} %get-tuple-element.13), kind=kOutput, calls=%fused_computation.4 | convolution fusion | flops 3222798336 | bytes 20709376 | tf_op jit(solution)/shard_map/dot_general | solution.py:27
  77.6 1.3 constant_dynamic-update-slice_fusion.8
  79.0 9.4 %fusion.21 = bf16[1,256,2048]{2,1,0:T(8,128)(2,1)} fusion(bf16[256,4096]{1,0:T(8,128)(2,1)S(1)} %constant_dynamic-update-slice_fusion.8, bf16[1,4096,2048]{2,1,0:T(8,128)(2,1)} %param.5), kind=kOutput, calls=%fused_computation.19 | convolution fusion | flops 4296015872 | bytes 19922944 | tf_op jit(solution)/shard_map/dot_general | solution.py:27
  88.4 2.4 %fusion.7 = f32[192,4096]{1,0:T(8,128)} fusion(f32[192,4096]{1,0:T(8,128)S(1)} %copy-done.4, bf16[256,4096]{1,0:T(8,128)(2,1)S(1)} %constant_dynamic-update-slice_fusion.8, bf16[96,256]{1,0:T(8,128)(2,1)S(1)} %copy-done.8, bf16[96,256]{1,0:T(8,128)(2,1)S(1)} %copy-done.7), kind=kOutput, calls=%fused_computation.9 | convolution fusion | flops 404422656 | bytes 8486912 | tf_op jit(solution)/shard_map/dot_general | solution.py:27
  90.8 3.4 %reduce_sum.49 = f32[96,4096]{1,0:T(8,128)} reduce(f32[2,96,4096]{2,1,0:T(8,128)} %bitcast.91, f32[]{:T(128)} %constant.67.clone.1), dimensions={0}, to_apply=%region_6.7 | reduce | flops 393216 | bytes 4718596 | tf_op jit(solution)/shard_map/reduce_sum | solution.py:31
  94.2 1.5 fusion.68
  96.1 1.5 %broadcast_multiply_fusion = bf16[256,4096]{1,0:T(8,128)(2,1)} fusion(bf16[256,4096]{1,0:T(8,128)(2,1)S(1)} %constant_dynamic-update-slice_fusion.8), kind=kLoop, calls=%fused_computation.44 | loop fusion | flops 1048576 | bytes 4194304 | tf_op jit(solution)/shard_map/mul | solution.py:116
  97.6 3.2 %collective-permute-done.6 = f16[32,2048]{1,0:T(8,128)(2,1)S(1)} collective-permute-done((f16[32,2048]{1,0:T(8,128)(2,1)S(1)}, f16[32,2048]{1,0:T(8,128)(2,1)S(1)}, u32[]{:S(2)}, u32[]{:S(2)}) %collective-permute-start.6) | collective-permute-done | bytes 131104 | tf_op jit(solution)/shard_map/ppermute | solution.py:14
  101.4 1.8 %collective-permute-start.9 = (f16[32,2048]{1,0:T(8,128)(2,1)S(1)}, f16[32,2048]{1,0:T(8,128)(2,1)S(1)}, u32[]{:S(2)}, u32[]{:S(2)}) collective-permute-start(f16[32,2048]{1,0:T(8,128)(2,1)S(1)} %dynamic-slice_convert_fusion.1), channel_id=1, source_target_pairs={{0,1},{1,0},{2,3},{3,2},{4,5},{5,4},{6,7},{7,6},{8,9},{9,8},{10,11... | collective-permute-start | bytes 393224 | tf_op jit(solution)/shard_map/ppermute | solution.py:14
  103.6 6.6 %collective-permute-done.9 = f16[32,2048]{1,0:T(8,128)(2,1)S(1)} collective-permute-done((f16[32,2048]{1,0:T(8,128)(2,1)S(1)}, f16[32,2048]{1,0:T(8,128)(2,1)S(1)}, u32[]{:S(2)}, u32[]{:S(2)}) %collective-permute-start.9) | collective-permute-done | bytes 131104 | tf_op jit(solution)/shard_map/ppermute | solution.py:14
  110.5 1.6 %collective-permute-start.10 = (f16[32,2048]{1,0:T(8,128)(2,1)S(1)}, f16[32,2048]{1,0:T(8,128)(2,1)S(1)}, u32[]{:S(2)}, u32[]{:S(2)}) collective-permute-start(f16[32,2048]{1,0:T(8,128)(2,1)S(1)} %get-tuple-element.33), channel_id=1, source_target_pairs={{0,4},{2,6},{4,0},{6,2},{8,12},{10,14},{12,8},{14,10},{16,20},{18,... | collective-permute-start | bytes 393224 | tf_op jit(solution)/shard_map/ppermute | solution.py:14
  112.5 3.1 %collective-permute-done.10 = f16[32,2048]{1,0:T(8,128)(2,1)S(1)} collective-permute-done((f16[32,2048]{1,0:T(8,128)(2,1)S(1)}, f16[32,2048]{1,0:T(8,128)(2,1)S(1)}, u32[]{:S(2)}, u32[]{:S(2)}) %collective-permute-start.10) | collective-permute-done | bytes 131104 | tf_op jit(solution)/shard_map/ppermute | solution.py:14
  116.0 1.6 %collective-permute-start.13 = (f16[32,2048]{1,0:T(8,128)(2,1)S(1)}, f16[32,2048]{1,0:T(8,128)(2,1)S(1)}, u32[]{:S(2)}, u32[]{:S(2)}) collective-permute-start(f16[32,2048]{1,0:T(8,128)(2,1)S(1)} %get-tuple-element.35), channel_id=1, source_target_pairs={{0,8},{2,10},{4,12},{6,14},{8,0},{10,2},{12,4},{14,6},{16,24},{18,... | collective-permute-start | bytes 393224 | tf_op jit(solution)/shard_map/ppermute | solution.py:14
  118.3 2.7 %collective-permute-done.13 = f16[32,2048]{1,0:T(8,128)(2,1)S(1)} collective-permute-done((f16[32,2048]{1,0:T(8,128)(2,1)S(1)}, f16[32,2048]{1,0:T(8,128)(2,1)S(1)}, u32[]{:S(2)}, u32[]{:S(2)}) %collective-permute-start.13) | collective-permute-done | bytes 131104 | tf_op jit(solution)/shard_map/ppermute | solution.py:14
  121.4 2.1 %collective-permute-done.11 = f16[32,2048]{1,0:T(8,128)(2,1)S(1)} collective-permute-done((f16[32,2048]{1,0:T(8,128)(2,1)S(1)}, f16[32,2048]{1,0:T(8,128)(2,1)S(1)}, u32[]{:S(2)}, u32[]{:S(2)}) %collective-permute-start.11) | collective-permute-done | bytes 131104 | tf_op jit(solution)/shard_map/ppermute | solution.py:14
  123.6 2.5 %collective-permute-done.14 = f16[32,2048]{1,0:T(8,128)(2,1)S(1)} collective-permute-done((f16[32,2048]{1,0:T(8,128)(2,1)S(1)}, f16[32,2048]{1,0:T(8,128)(2,1)S(1)}, u32[]{:S(2)}, u32[]{:S(2)}) %collective-permute-start.14) | collective-permute-done | bytes 131104 | tf_op jit(solution)/shard_map/ppermute | solution.py:14
  126.1 1.6 %reduce-precision_convert_fusion = (bf16[96,4096]{1,0:T(8,128)(2,1)}, bf16[96,4096]{1,0:T(8,128)(2,1)}) fusion(f16[32,4096]{1,0:T(8,128)(2,1)S(1)} %constant_dynamic-update-slice_fusion, f16[32,4096]{1,0:T(8,128)(2,1)S(1)} %constant_dynamic-update-slice_fusion.2, f16[32,4096]{1,0:T(8,128)(2,1)S(1)} %constant_dynamic-update-slice_fusion.4), kind=kLoop, calls=%fused_computation.24 | loop fusion | flops 3538944 | bytes 2359296 | tf_op jit(solution)/shard_map/convert_element_type | solution.py:21
  127.7 20.0 %fusion = bf16[1,4096,2048]{2,1,0:T(8,128)(2,1)} fusion(bf16[1,4096,2048]{2,1,0:T(8,128)(2,1)} %param.5, bf16[96,4096]{1,0:T(8,128)(2,1)} %get-tuple-element.12, bf16[96,4096]{1,0:T(8,128)(2,1)} %get-tuple-element.11, bf16[256,4096]{1,0:T(8,128)(2,1)S(1)} %copy-done.5, bf16[96,2048]{1,0:T(8,128)(2,1)S(1)} %get-tuple-element.13, ...), kind=kOutput, calls=%fused_computation.1 | convolution fusion | flops 9178710016 | bytes 39059456 | tf_op jit(solution)/shard_map/dot_general | solution.py:27
  (92 shorter events, 12.9 us)
Async XLA Ops:
  0.6 1.4 copy-start
  2.5 11.7 %collective-permute-start.1 = (f32[32,128]{1,0:T(8,128)S(1)}, f32[32,128]{1,0:T(8,128)S(1)}, u32[]{:S(2)}, u32[]{:S(2)}) collective-permute-start(f32[32,128]{1,0:T(8,128)S(1)} %convolution_reduce_fusion.2), channel_id=1, source_target_pairs={{0,1},{1,0},{2,3},{3,2},{4,5},{5,4},{6,7},{7,6},{8,9},{9,8},{10,11... | collective-permute-start | bytes 49160 | tf_op jit(solution)/shard_map/ppermute | solution.py:14
  5.5 8.7 %copy-start.1 = (bf16[1,256,2048]{2,1,0:T(8,128)(2,1)S(1)}, bf16[1,256,2048]{2,1,0:T(8,128)(2,1)}, u32[]{:S(2)}) copy-start(bf16[1,256,2048]{2,1,0:T(8,128)(2,1)} %param.6) | copy-start | bytes 3145732
  14.6 1.6 %collective-permute-start.2 = (f32[32,2048]{1,0:T(8,128)S(1)}, f32[32,2048]{1,0:T(8,128)S(1)}, u32[]{:S(2)}, u32[]{:S(2)}) collective-permute-start(f32[32,2048]{1,0:T(8,128)S(1)} %multiply_subtract_fusion), channel_id=1, source_target_pairs={{0,2},{2,0},{4,6},{6,4},{8,10},{10,8},{12,14},{14,12},{16,18},{18,... | collective-permute-start | bytes 786440 | tf_op jit(solution)/shard_map/ppermute | solution.py:14
  14.6 63.0 %collective-permute-start = (bf16[128,4096]{1,0:T(8,128)(2,1)S(1)}, bf16[128,4096]{1,0:T(8,128)(2,1)}, u32[]{:S(2)}, u32[]{:S(2)}) collective-permute-start(bf16[128,4096]{1,0:T(8,128)(2,1)S(1)} %bitcast.94), channel_id=1, source_target_pairs={{0,1},{1,0},{2,3},{3,2},{4,5},{5,4},{6,7},{7,6},{8,9},{9,8},{10,11... | collective-permute-start | bytes 3145736 | tf_op jit(solution)/shard_map/ppermute | solution.py:14
  16.9 8.3 %collective-permute-start.3 = (f32[32,2048]{1,0:T(8,128)S(1)}, f32[32,2048]{1,0:T(8,128)S(1)}, u32[]{:S(2)}, u32[]{:S(2)}) collective-permute-start(f32[32,2048]{1,0:T(8,128)S(1)} %get-tuple-element.16), channel_id=1, source_target_pairs={{0,4},{2,6},{4,0},{6,2},{8,12},{10,14},{12,8},{14,10},{16,20},{18,... | collective-permute-start | bytes 786440 | tf_op jit(solution)/shard_map/ppermute | solution.py:14
  26.0 7.7 %collective-permute-start.4 = (f32[32,2048]{1,0:T(8,128)S(1)}, f32[32,2048]{1,0:T(8,128)}, u32[]{:S(2)}, u32[]{:S(2)}) collective-permute-start(f32[32,2048]{1,0:T(8,128)S(1)} %get-tuple-element.18), channel_id=1, source_target_pairs={{0,8},{2,10},{4,12},{6,14},{8,0},{10,2},{12,4},{14,6},{16,24},{18,... | collective-permute-start | bytes 786440 | tf_op jit(solution)/shard_map/ppermute | solution.py:14
  36.8 4.5 %collective-permute-start.5 = (f32[96,96]{1,0:T(8,128)S(1)}, f32[96,96]{1,0:T(8,128)S(1)}, u32[]{:S(2)}, u32[]{:S(2)}) collective-permute-start(f32[96,96]{1,0:T(8,128)S(1)} %fusion.66), channel_id=1, source_target_pairs={{0,1},{1,0},{2,3},{3,2},{4,5},{5,4},{6,7},{7,6},{8,9},{9,8},{10,11... | collective-permute-start | bytes 110600 | tf_op jit(solution)/shard_map/ppermute | solution.py:14
  60.9 2.2 %copy-start.2 = (bf16[1,256,2048]{2,1,0:T(8,128)(2,1)S(1)}, bf16[1,256,2048]{2,1,0:T(8,128)(2,1)}, u32[]{:S(2)}) copy-start(bf16[1,256,2048]{2,1,0:T(8,128)(2,1)} %param.6) | copy-start | bytes 3145732
  63.0 0.8 copy-start.6
  79.0 9.4 %copy-start.4 = (f32[192,4096]{1,0:T(8,128)S(1)}, f32[192,4096]{1,0:T(8,128)}, u32[]{:S(2)}) copy-start(f32[192,4096]{1,0:T(8,128)} %fusion.3) | copy-start | bytes 9437188
  79.0 9.4 %copy-start.7 = (bf16[96,256]{1,0:T(8,128)(2,1)S(1)}, bf16[96,256]{1,0:T(8,128)(2,1)}, u32[]{:S(2)}) copy-start(bf16[96,256]{1,0:T(8,128)(2,1)} %get-tuple-element.28) | copy-start | bytes 147460
  79.0 9.4 %copy-start.8 = (bf16[96,256]{1,0:T(8,128)(2,1)S(1)}, bf16[96,256]{1,0:T(8,128)(2,1)}, u32[]{:S(2)}) copy-start(bf16[96,256]{1,0:T(8,128)(2,1)} %get-tuple-element.29) | copy-start | bytes 147460
  95.7 5.1 %collective-permute-start.6 = (f16[32,2048]{1,0:T(8,128)(2,1)S(1)}, f16[32,2048]{1,0:T(8,128)(2,1)S(1)}, u32[]{:S(2)}, u32[]{:S(2)}) collective-permute-start(f16[32,2048]{1,0:T(8,128)(2,1)S(1)} %dynamic-slice_convert_fusion.2), channel_id=1, source_target_pairs={{0,1},{1,0},{2,3},{3,2},{4,5},{5,4},{6,7},{7,6},{8,9},{9,8},{10,11... | collective-permute-start | bytes 393224 | tf_op jit(solution)/shard_map/ppermute | solution.py:14
  97.6 12.6 %copy-start.9 = (f32[32,32]{1,0:T(8,128)S(1)}, f32[32,32]{1,0:T(8,128)}, u32[]{:S(2)}) copy-start(f32[32,32]{1,0:T(8,128)} %fusion.58) | copy-start | bytes 12292
  97.6 14.5 %copy-start.10 = (f32[32,32]{1,0:T(8,128)S(1)}, f32[32,32]{1,0:T(8,128)}, u32[]{:S(2)}) copy-start(f32[32,32]{1,0:T(8,128)} %fusion.57) | copy-start | bytes 12292
  100.9 2.3 %collective-permute-start.7 = (f32[32,2048]{1,0:T(8,128)S(1)}, f32[32,2048]{1,0:T(8,128)S(1)}, u32[]{:S(2)}, u32[]{:S(2)}) collective-permute-start(f32[32,2048]{1,0:T(8,128)S(1)} %convert_add_fusion.1), channel_id=1, source_target_pairs={{0,2},{2,0},{4,6},{6,4},{8,10},{10,8},{12,14},{14,12},{16,18},{18,... | collective-permute-start | bytes 786440 | tf_op jit(solution)/shard_map/ppermute | solution.py:14
  101.0 11.5 %collective-permute-start.12 = (f16[32,2048]{1,0:T(8,128)(2,1)S(1)}, f16[32,2048]{1,0:T(8,128)(2,1)S(1)}, u32[]{:S(2)}, u32[]{:S(2)}) collective-permute-start(f16[32,2048]{1,0:T(8,128)(2,1)S(1)} %dynamic-slice_convert_fusion), channel_id=1, source_target_pairs={{0,1},{1,0},{2,3},{3,2},{4,5},{5,4},{6,7},{7,6},{8,9},{9,8},{10,11... | collective-permute-start | bytes 393224 | tf_op jit(solution)/shard_map/ppermute | solution.py:14
  101.4 8.8 %collective-permute-start.9 = (f16[32,2048]{1,0:T(8,128)(2,1)S(1)}, f16[32,2048]{1,0:T(8,128)(2,1)S(1)}, u32[]{:S(2)}, u32[]{:S(2)}) collective-permute-start(f16[32,2048]{1,0:T(8,128)(2,1)S(1)} %dynamic-slice_convert_fusion.1), channel_id=1, source_target_pairs={{0,1},{1,0},{2,3},{3,2},{4,5},{5,4},{6,7},{7,6},{8,9},{9,8},{10,11... | collective-permute-start | bytes 393224 | tf_op jit(solution)/shard_map/ppermute | solution.py:14
  103.3 15.1 %collective-permute-start.8 = (f16[32,2048]{1,0:T(8,128)(2,1)S(1)}, f16[32,2048]{1,0:T(8,128)(2,1)S(1)}, u32[]{:S(2)}, u32[]{:S(2)}) collective-permute-start(f16[32,2048]{1,0:T(8,128)(2,1)S(1)} %get-tuple-element.3), channel_id=1, source_target_pairs={{0,1},{1,0},{2,3},{3,2},{4,5},{5,4},{6,7},{7,6},{8,9},{9,8},{10,11... | collective-permute-start | bytes 393224 | tf_op jit(solution)/shard_map/ppermute | solution.py:14
  110.5 5.0 %collective-permute-start.10 = (f16[32,2048]{1,0:T(8,128)(2,1)S(1)}, f16[32,2048]{1,0:T(8,128)(2,1)S(1)}, u32[]{:S(2)}, u32[]{:S(2)}) collective-permute-start(f16[32,2048]{1,0:T(8,128)(2,1)S(1)} %get-tuple-element.33), channel_id=1, source_target_pairs={{0,4},{2,6},{4,0},{6,2},{8,12},{10,14},{12,8},{14,10},{16,20},{18,... | collective-permute-start | bytes 393224 | tf_op jit(solution)/shard_map/ppermute | solution.py:14
  116.0 5.0 %collective-permute-start.13 = (f16[32,2048]{1,0:T(8,128)(2,1)S(1)}, f16[32,2048]{1,0:T(8,128)(2,1)S(1)}, u32[]{:S(2)}, u32[]{:S(2)}) collective-permute-start(f16[32,2048]{1,0:T(8,128)(2,1)S(1)} %get-tuple-element.35), channel_id=1, source_target_pairs={{0,8},{2,10},{4,12},{6,14},{8,0},{10,2},{12,4},{14,6},{16,24},{18,... | collective-permute-start | bytes 393224 | tf_op jit(solution)/shard_map/ppermute | solution.py:14
  117.6 10.1 %copy-start.3 = (bf16[1,256,2048]{2,1,0:T(8,128)(2,1)S(1)}, bf16[1,256,2048]{2,1,0:T(8,128)(2,1)}, u32[]{:S(2)}) copy-start(bf16[1,256,2048]{2,1,0:T(8,128)(2,1)} %param.6) | copy-start | bytes 3145732
  117.6 10.1 %copy-start.5 = (bf16[256,4096]{1,0:T(8,128)(2,1)S(1)}, bf16[256,4096]{1,0:T(8,128)(2,1)}, u32[]{:S(2)}) copy-start(bf16[256,4096]{1,0:T(8,128)(2,1)} %broadcast_multiply_fusion) | copy-start | bytes 6291460
  117.7 5.8 %collective-permute-start.11 = (f16[32,2048]{1,0:T(8,128)(2,1)S(1)}, f16[32,2048]{1,0:T(8,128)(2,1)S(1)}, u32[]{:S(2)}, u32[]{:S(2)}) collective-permute-start(f16[32,2048]{1,0:T(8,128)(2,1)S(1)} %get-tuple-element.5), channel_id=1, source_target_pairs={{0,1},{1,0},{2,3},{3,2},{4,5},{5,4},{6,7},{7,6},{8,9},{9,8},{10,11... | collective-permute-start | bytes 393224 | tf_op jit(solution)/shard_map/ppermute | solution.py:14
  121.1 5.0 %collective-permute-start.14 = (f16[32,2048]{1,0:T(8,128)(2,1)S(1)}, f16[32,2048]{1,0:T(8,128)(2,1)S(1)}, u32[]{:S(2)}, u32[]{:S(2)}) collective-permute-start(f16[32,2048]{1,0:T(8,128)(2,1)S(1)} %get-tuple-element.7), channel_id=1, source_target_pairs={{0,1},{1,0},{2,3},{3,2},{4,5},{5,4},{6,7},{7,6},{8,9},{9,8},{10,11... | collective-permute-start | bytes 393224 | tf_op jit(solution)/shard_map/ppermute | solution.py:14

commit v2 on v1

--- a/solution.py
+++ b/solution.py
@@ -1,6 +1,10 @@
+import functools
+
 import jax
 import jax.numpy as jnp
 from jax import lax
+from jax.experimental import pallas as pl
+from jax.experimental.pallas import tpu as pltpu
 from jax.sharding import PartitionSpec as P
 
 STEPS = 3
@@ -62,6 +66,66 @@
     return mine + partner(theirs.astype(F16), "tp", 0).astype(F32)
 
 
+def parts(x):
+    high = x.astype(BF16)
+    return high, (x - high.astype(F32)).astype(BF16)
+
+
+def limits(mib):
+    return pltpu.CompilerParams(vmem_limit_bytes=mib * 1024 * 1024)
+
+
+def factor_kernel(rank, gram_ref, diff_ref, o_ref, cross_ref):
+    row = lax.broadcasted_iota(jnp.int32, (rank, rank), 0)
+    col = lax.broadcasted_iota(jnp.int32, (rank, rank), 1)
+    unit = (row == col).astype(F32)
+    gram = [[gram_ref[s * rank:(s + 1) * rank, t * rank:(t + 1) * rank] for t in range(s + 1)] for s in range(STEPS)]
+    rest = [gram[s][s] for s in range(STEPS)]
+    inv = [unit] * STEPS
+    for k in range(rank - 1):
+        for s in range(STEPS):
+            pivot = rest[s][k:k + 1, :]
+            ratio = rest[s][:, k:k + 1] / pivot[:, k:k + 1]
+            ratio = jnp.where(row > k, jnp.broadcast_to(ratio, (rank, rank)), 0.0)
+            inv[s] = inv[s] - ratio * inv[s][k:k + 1, :]
+            rest[s] = rest[s] - ratio * pivot
+    for s in range(STEPS):
+        pivots = jnp.sum(rest[s] * unit, axis=1, keepdims=True)
+        inv[s] = inv[s] / jnp.sqrt(pivots)
+        rows = pl.ds(s * rank, rank)
+        ortho = jnp.dot(inv[s], diff_ref[rows, :], precision=HIGH, preferred_element_type=F32)
+        high, low = parts(ortho)
+        o_ref[rows, :] = high
+        o_ref[pl.ds((STEPS + s) * rank, rank), :] = low
+        o_ref[pl.ds((2 * STEPS + s) * rank, rank), :] = high
+        for t in range(STEPS):
+            if t < s:
+                half = jnp.dot(inv[s], gram[s][t], precision=HIGH, preferred_element_type=F32)
+                cross_ref[s, t] = lax.dot_general(
+                    half, inv[t], (((1,), (1,)), ((), ())), precision=HIGH, preferred_element_type=F32)
+            else:
+                cross_ref[s, t] = jnp.zeros((rank, rank), F32)
+
+
+def input_kernel(count, factor, o_ref, c_ref, full_ref, w_ref, x_ref, co_ref):
+    @pl.when(pl.program_id(0) == 0)
+    def _():
+        both = dot(o_ref[...], c_ref[...], 1, 1)
+        high, low = parts(both[:count] + both[count:])
+        co_ref[:count, :] = high
+        co_ref[count:, :] = low
+
+    both = dot(o_ref[...], w_ref[...], 1, 1) - factor * dot(co_ref[...], full_ref[...], 1, 0)
+    x_ref[...] = both[:count] + both[count:]
+
+
+def update_kernel(factor, full_ref, b_ref, c_ref, o_ref, w_ref, new_ref):
+    high, low = parts(-0.5 * b_ref[...])
+    left = jnp.concatenate([high, high, low], 0)
+    change = dot(full_ref[...] * jnp.asarray(-factor, BF16), c_ref[...], 0, 0) + dot(left, o_ref[...], 0, 0)
+    new_ref[...] = (w_ref[...].astype(F32) + change).astype(BF16)
+
+
 def shards(acts, weights, cotangent, start_factors):
     d, rank = start_factors.shape
     scale = d ** (-0.5)
@@ -81,24 +145,31 @@
         side = 0.5 * (side + other)
     diff = jnp.concatenate(diffs, 0)
     gram = total(lax.dot_general(diff, diff, (((1,), (1,)), ((), ())), precision=HIGH))
-    blocks = gram.reshape(STEPS, rank, STEPS, rank)
-    lower = jnp.linalg.cholesky(jnp.stack([blocks[s, :, s] for s in range(STEPS)]))
-    eye = jnp.broadcast_to(jnp.eye(rank, dtype=F32), lower.shape)
-    inv = lax.linalg.triangular_solve(lower, eye, left_side=True, lower=True)
-    ortho = jnp.einsum("skl,slo->sko", inv, diff.reshape(STEPS, rank, -1), precision=HIGH)
-    ortho = ortho.reshape(STEPS * rank, -1)
-    cross = {}
-    for s in range(STEPS):
-        for t in range(s):
-            half = jnp.dot(inv[s], blocks[s, :, t], precision=HIGH)
-            cross[s, t] = jnp.dot(half, inv[t].T, precision=HIGH)
-
-    o_hi, o_lo = split(ortho, 2)
-    o2 = jnp.concatenate([o_hi, o_lo], 0)
-    co = folded(dot(o2, c, 1, 1), 2)
-    co2 = jnp.concatenate(split(co, 2), 0)
-    x = folded(dot(o2, w, 1, 1) - 0.5 * scale * dot(co2, full, 1, 0), 2)
-
+    count = STEPS * rank
+    width, tokens = w.shape[1], full.shape[0]
+    o3, cross = pl.pallas_call(
+        functools.partial(factor_kernel, rank),
+        out_shape=(jax.ShapeDtypeStruct((3 * count, width), BF16), jax.ShapeDtypeStruct((STEPS, STEPS, rank, rank), F32)),
+        compiler_params=limits(16),
+        name="factor",
+    )(gram, diff)
+
+    tile = 512
+    x = pl.pallas_call(
+        functools.partial(input_kernel, count, 0.5 * scale),
+        grid=(d // tile,),
+        in_specs=[
+            pl.BlockSpec((2 * count, width), lambda i: (0, 0)),
+            pl.BlockSpec((tokens, width), lambda i: (0, 0)),
+            pl.BlockSpec((tokens, tile), lambda i: (0, i)),
+            pl.BlockSpec((tile, width), lambda i: (i, 0)),
+        ],
+        out_specs=pl.BlockSpec((count, tile), lambda i: (0, i)),
+        out_shape=jax.ShapeDtypeStruct((count, d), F32),
+        scratch_shapes=[pltpu.VMEM((2 * count, tokens), BF16)],
+        compiler_params=limits(24),
+        name="input_side",
+    )(o3, c, full, w)
     backs = []
     for step in range(STEPS):
         local = scattered(x[step * rank:(step + 1) * rank])
@@ -109,13 +180,27 @@
         else:
             other = partner(local.astype(F16), "rep", step).astype(F32)
         backs.append(local + other)
+        if step == 0:
+            late, backs[0] = lax.optimization_barrier((full, backs[0]))
     back = jnp.concatenate([gather(b.astype(F16), 1).astype(F32) for b in backs], 0)
 
-    projected = (dot(full, w, 1, 0) * scale).astype(BF16)[None]
-    b_hi, b_lo = split(-0.5 * back, 2)
-    left = jnp.concatenate([full * jnp.asarray(-0.5 * scale, BF16), b_hi, b_hi, b_lo], 0)
-    right = jnp.concatenate([c, o_hi, o_lo, o_hi], 0)
-    new = (w.astype(F32) + dot(left, right, 0, 0)).astype(BF16)[None]
+    projected = (dot(late, w, 1, 0) * scale).astype(BF16)[None]
+    tile = 256
+    new = pl.pallas_call(
+        functools.partial(update_kernel, 0.5 * scale),
+        grid=(d // tile,),
+        in_specs=[
+            pl.BlockSpec((tokens, tile), lambda i: (0, i)),
+            pl.BlockSpec((count, tile), lambda i: (0, i)),
+            pl.BlockSpec((tokens, width), lambda i: (0, 0)),
+            pl.BlockSpec((3 * count, width), lambda i: (0, 0)),
+            pl.BlockSpec((tile, width), lambda i: (i, 0)),
+        ],
+        out_specs=pl.BlockSpec((tile, width), lambda i: (i, 0)),
+        out_shape=jax.ShapeDtypeStruct(w.shape, BF16),
+        compiler_params=limits(24),
+        name="update",
+    )(full, back, c, o3, w)[None]
     return projected, new
 
 

time: 148 us -> 121 us (0.82)
  matrix products: 62.5 us -> 24.7 us
  Pallas kernels: 0 us -> 29.8 us
  other arithmetic: 30 us -> 6.19 us
  local copies, waits for them, and re-layouts: 4.06 us -> 10.2 us
  waiting for transfers between devices: 36 us -> 32.8 us
    dot_general x8 -> x4, matrix products: 54.9 us -> 21.6 us  [dot(): lax.dot_general(a, b, (((ca,), (cb,)), ((), ())), preferred_element_type=...]
    pallas_call x0 -> x3, Pallas kernels: none -> 29.8 us  [the longest x1 17.7 us: shards(): pl.pallas_call(functools.partial(update_kernel, 0.5 * scale), grid=(d //...]
    another operation x8 -> x0, other arithmetic: 16.6 us -> none  [the longest x4 9.14 us: shards(): jnp.linalg.cholesky(jnp.stack([blocks[s, :, s] for s in range(STEPS)]))]
    unnamed x25 -> x24, local copies, waits for them, and re-layouts: 0.47 us -> 5.82 us
    dot_general x7 -> x0, matrix products: 4.11 us -> none  [the longest x1 2 us: shards(): jnp.einsum('skl,slo->sko', inv, diff.reshape(STEPS, rank, -1), precision=...]
    reduce_sum x1 -> x0, other arithmetic: 3.43 us -> none  [folded(): return out.reshape((terms, -1) + out.shape[1:]).sum(0)]
    ppermute x15, waiting for transfers between devices: 36 us -> 32.8 us  [partner(): return lax.ppermute(block, axis, route)]
    convert_element_type x5 -> x2, other arithmetic: 3.59 us -> 1.17 us  [split(): out.append(part.astype(BF16))]
  transfers between devices with their start and end apart: 15 -> 15, of which waited for: 10 -> 8; matrix products, arithmetic and copies ran while one was open for 37% -> 24% of each run, Pallas kernels for 0% -> 3%
where the time goes in v2:
time: 121 us; the launch traced here: 120 us
  waiting for transfers between devices  32.8 us (27%)
  Pallas kernels  29.8 us (25%)
  matrix products  24.7 us (20%)
  starting transfers between devices  15.4 us (13%)
  local copies, waits for them, and re-layouts  10.2 us (8%)
  other arithmetic  6.19 us (5%)
    ppermute x15, waiting for transfers between devices, partner(): return lax.ppermute(block, axis, route)  32.8 us
    dot_general x4, matrix products, dot(): lax.dot_general(a, b, (((ca,), (cb,)), ((), ())), preferred_element_type=...  21.6 us
    pallas_call x1, Pallas kernels, shards(): pl.pallas_call(functools.partial(update_kernel, 0.5 * scale), grid=(d //...  17.7 us
    ppermute x15, starting transfers between devices, partner(): return lax.ppermute(block, axis, route)  15.4 us
    pallas_call x1, Pallas kernels, shards(): pl.pallas_call(functools.partial(input_kernel, count, 0.5 * scale), grid=...  8.14 us
    unnamed x24, local copies, waits for them, and re-layouts  5.82 us
    pallas_call x1, Pallas kernels, shards(): pl.pallas_call(functools.partial(factor_kernel, rank), out_shape=(jax.Sha...  4.02 us
    sub x3, other arithmetic, shards(): diffs.append(side - other)  2.46 us
  transfers between devices with their start and end apart: 15, of which 8 were waited for; matrix products, arithmetic and copies ran while one was open for 24% of the time, Pallas kernels for 3%

profile of v2, /device:TPU:0, one launch (start us, length us, event | category | flops | bytes accessed | tf_op | source)
XLA Modules:
  0.0 120.3 jit_solution(6118267985669532610)
XLA Ops:
  0.6 1.2 reduce-precision_convert_fusion.1
  1.9 1.7 %convolution_reduce_fusion.1 = f32[32,128]{1,0:T(8,128)S(1)} fusion(bf16[3,32,4096]{2,1,0:T(8,128)(2,1)S(1)} %bitcast.55, bf16[1,128,4096]{2,1,0:T(8,128)(2,1)} %param.4), kind=kOutput, calls=%fused_computation.10 | convolution fusion | flops 100671488 | bytes 1851392 | tf_op jit(solution)/shard_map/dot_general | solution.py:31
  3.6 3.0 %collective-permute-start.1 = (f32[32,128]{1,0:T(8,128)S(1)}, f32[32,128]{1,0:T(8,128)S(1)}, u32[]{:S(2)}, u32[]{:S(2)}) collective-permute-start(f32[32,128]{1,0:T(8,128)S(1)} %convolution_reduce_fusion.1), channel_id=1, source_target_pairs={{0,1},{1,0},{2,3},{3,2},{4,5},{5,4},{6,7},{7,6},{8,9},{9,8},{10,11... | collective-permute-start | bytes 49160 | tf_op jit(solution)/shard_map/ppermute | solution.py:18
  6.6 8.6 %fusion.4 = f32[32,2048]{1,0:T(8,128)S(1)} fusion(bf16[3,32,4096]{2,1,0:T(8,128)(2,1)S(1)} %bitcast.56, bf16[1,4096,2048]{2,1,0:T(8,128)(2,1)} %param.5), kind=kOutput, calls=%fused_computation.9 | convolution fusion | flops 1610743808 | bytes 17825792 | tf_op jit(solution)/shard_map/dot_general | solution.py:31
  15.7 1.5 %collective-permute-done.2 = f32[32,2048]{1,0:T(8,128)S(1)} collective-permute-done((f32[32,2048]{1,0:T(8,128)S(1)}, f32[32,2048]{1,0:T(8,128)S(1)}, u32[]{:S(2)}, u32[]{:S(2)}) %collective-permute-start.2) | collective-permute-done | bytes 262176 | tf_op jit(solution)/shard_map/ppermute | solution.py:18
  17.2 0.7 fusion.24
  18.0 1.5 %collective-permute-start.3 = (f32[32,2048]{1,0:T(8,128)S(1)}, f32[32,2048]{1,0:T(8,128)S(1)}, u32[]{:S(2)}, u32[]{:S(2)}) collective-permute-start(f32[32,2048]{1,0:T(8,128)S(1)} %get-tuple-element.20), channel_id=1, source_target_pairs={{0,4},{2,6},{4,0},{6,2},{8,12},{10,14},{12,8},{14,10},{16,20},{18,... | collective-permute-start | bytes 786440 | tf_op jit(solution)/shard_map/ppermute | solution.py:18
  20.0 6.3 %collective-permute-done.3 = f32[32,2048]{1,0:T(8,128)S(1)} collective-permute-done((f32[32,2048]{1,0:T(8,128)S(1)}, f32[32,2048]{1,0:T(8,128)S(1)}, u32[]{:S(2)}, u32[]{:S(2)}) %collective-permute-start.3) | collective-permute-done | bytes 262176 | tf_op jit(solution)/shard_map/ppermute | solution.py:18
  26.3 0.7 fusion.25
  27.1 1.6 %collective-permute-start.4 = (f32[32,2048]{1,0:T(8,128)S(1)}, f32[32,2048]{1,0:T(8,128)}, u32[]{:S(2)}, u32[]{:S(2)}) collective-permute-start(f32[32,2048]{1,0:T(8,128)S(1)} %get-tuple-element.22), channel_id=1, source_target_pairs={{0,8},{2,10},{4,12},{6,14},{8,0},{10,2},{12,4},{14,6},{16,24},{18,... | collective-permute-start | bytes 786440 | tf_op jit(solution)/shard_map/ppermute | solution.py:18
  28.9 1.3 %constant_dynamic-update-slice_fusion.9 = bf16[256,4096]{1,0:T(8,128)(2,1)S(1)} fusion(bf16[256,4096]{1,0:T(8,128)(2,1)S(1)} %broadcast_in_dim.12, s32[]{:T(128)S(6)} %select_n.8, bf16[1,128,4096]{2,1,0:T(8,128)(2,1)} %param.4), kind=kLoop, calls=%fused_computation.56 | loop fusion | bytes 2097156 | tf_op jit(solution)/shard_map/dynamic_update_slice | solution.py:48
  30.2 4.6 %collective-permute-done.4 = f32[32,2048]{1,0:T(8,128)} collective-permute-done((f32[32,2048]{1,0:T(8,128)S(1)}, f32[32,2048]{1,0:T(8,128)}, u32[]{:S(2)}, u32[]{:S(2)}) %collective-permute-start.4) | collective-permute-done | bytes 262176 | tf_op jit(solution)/shard_map/ppermute | solution.py:18
  34.8 1.0 sub.51
  35.8 2.0 %fusion.21 = f32[96,96]{1,0:T(8,128)S(1)} fusion(f32[32,2048]{1,0:T(8,128)S(1)} %sub.51, f32[32,2048]{1,0:T(8,128)} %get-tuple-element.21, f32[32,2048]{1,0:T(8,128)} %get-tuple-element.19), kind=kOutput, calls=%fused_computation.58 | convolution fusion | flops 226885632 | bytes 823296 | tf_op jit(solution)/shard_map/dot_general | solution.py:147
  37.8 0.7 collective-permute-start.5
  38.5 1.1 pad_maximum_fusion.1.diff_ref
  39.6 6.1 %collective-permute-done.5 = f32[96,96]{1,0:T(8,128)S(1)} collective-permute-done((f32[96,96]{1,0:T(8,128)S(1)}, f32[96,96]{1,0:T(8,128)S(1)}, u32[]{:S(2)}, u32[]{:S(2)}) %collective-permute-start.5) | collective-permute-done | bytes 36896 | tf_op jit(solution)/shard_map/ppermute | solution.py:18
  45.7 4.0 %factor.1 = (bf16[288,2048]{1,0:T(8,128)(2,1)S(1)}, f32[3,3,32,32]{3,2,1,0:T(8,128)S(1)}) custom-call(f32[96,96]{1,0:T(8,128)S(1)} %add.55.gram_ref, f32[96,2048]{1,0:T(8,128)S(1)} %pad_maximum_fusion.1.diff_ref), custom_call_target="tpu_custom_call" | custom-call | tf_op jit(solution)/shard_map/factor/pallas_call | solution.py:150
  49.7 1.8 %constant_dynamic-update-slice_fusion.8.full_ref = bf16[256,4096]{1,0:T(8,128)(2,1)S(1)} fusion(bf16[256,4096]{1,0:T(8,128)(2,1)S(1)} %constant_dynamic-update-slice_fusion.9, bf16[128,4096]{1,0:T(8,128)(2,1)} %collective-permute-done, s32[]{:T(128)S(6)} %select_n.9), kind=kLoop, calls=%fused_computation.55 | loop fusion | bytes 2097156 | tf_op jit(solution)/shard_map/dynamic_update_slice | solution.py:49
  51.5 5.8 %copy-done = bf16[1,4096,2048]{2,1,0:T(8,128)(2,1)S(1)} copy-done((bf16[1,4096,2048]{2,1,0:T(8,128)(2,1)S(1)}, bf16[1,4096,2048]{2,1,0:T(8,128)(2,1)}, u32[]{:S(2)}) %copy-start) | copy-done | bytes 16777240
  57.3 8.1 %input_side.1 = f32[96,4096]{1,0:T(8,128)S(1)} custom-call(bf16[288,2048]{1,0:T(8,128)(2,1)S(1)} %get-tuple-element.6.o_ref, bf16[256,2048]{1,0:T(8,128)(2,1)S(1)} %bitcast.52, bf16[256,4096]{1,0:T(8,128)(2,1)S(1)} %constant_dynamic-update-slice_fusion.8.full_ref, bf16[4096,2048]{1,0:T(8,128)(2,1)S(1)} %bitcast.48), custom_call_target="tpu_custom_call" | custom-call | tf_op jit(solution)/shard_map/input_side/pallas_call | solution.py:158
  65.4 0.9 fusion.23
  67.0 4.4 %collective-permute-done.6 = f16[32,2048]{1,0:T(8,128)(2,1)S(1)} collective-permute-done((f16[32,2048]{1,0:T(8,128)(2,1)S(1)}, f16[32,2048]{1,0:T(8,128)(2,1)S(1)}, u32[]{:S(2)}, u32[]{:S(2)}) %collective-permute-start.6) | collective-permute-done | bytes 131104 | tf_op jit(solution)/shard_map/ppermute | solution.py:18
  71.5 1.0 dynamic-slice_convert_fusion.1
  73.1 1.6 %collective-permute-start.12 = (f16[32,2048]{1,0:T(8,128)(2,1)S(1)}, f16[32,2048]{1,0:T(8,128)(2,1)S(1)}, u32[]{:S(2)}, u32[]{:S(2)}) collective-permute-start(f16[32,2048]{1,0:T(8,128)(2,1)S(1)} %dynamic-slice_convert_fusion), channel_id=1, source_target_pairs={{0,1},{1,0},{2,3},{3,2},{4,5},{5,4},{6,7},{7,6},{8,9},{9,8},{10,11... | collective-permute-start | bytes 393224 | tf_op jit(solution)/shard_map/ppermute | solution.py:18
  75.4 3.5 %collective-permute-done.9 = f16[32,2048]{1,0:T(8,128)(2,1)S(1)} collective-permute-done((f16[32,2048]{1,0:T(8,128)(2,1)S(1)}, f16[32,2048]{1,0:T(8,128)(2,1)S(1)}, u32[]{:S(2)}, u32[]{:S(2)}) %collective-permute-start.9) | collective-permute-done | bytes 131104 | tf_op jit(solution)/shard_map/ppermute | solution.py:18
  79.9 11.0 %fusion.3 = bf16[1,256,2048]{2,1,0:T(8,128)(2,1)} fusion(bf16[256,4096]{1,0:T(8,128)(2,1)S(1)} %constant_dynamic-update-slice_fusion.8.full_ref, bf16[1,4096,2048]{2,1,0:T(8,128)(2,1)} %param.5), kind=kOutput, calls=%fused_computation.4 | convolution fusion | flops 4296015872 | bytes 19922944 | tf_op jit(solution)/shard_map/dot_general | solution.py:31
  92.1 1.9 %collective-permute-start.13 = (f16[32,2048]{1,0:T(8,128)(2,1)S(1)}, f16[32,2048]{1,0:T(8,128)(2,1)S(1)}, u32[]{:S(2)}, u32[]{:S(2)}) collective-permute-start(f16[32,2048]{1,0:T(8,128)(2,1)S(1)} %get-tuple-element.31), channel_id=1, source_target_pairs={{0,8},{2,10},{4,12},{6,14},{8,0},{10,2},{12,4},{14,6},{16,24},{18,... | collective-permute-start | bytes 393224 | tf_op jit(solution)/shard_map/ppermute | solution.py:18
  94.0 3.1 %collective-permute-done.13 = f16[32,2048]{1,0:T(8,128)(2,1)S(1)} collective-permute-done((f16[32,2048]{1,0:T(8,128)(2,1)S(1)}, f16[32,2048]{1,0:T(8,128)(2,1)S(1)}, u32[]{:S(2)}, u32[]{:S(2)}) %collective-permute-start.13) | collective-permute-done | bytes 131104 | tf_op jit(solution)/shard_map/ppermute | solution.py:18
  97.3 1.8 %collective-permute-start.14 = (f16[32,2048]{1,0:T(8,128)(2,1)S(1)}, f16[32,2048]{1,0:T(8,128)(2,1)S(1)}, u32[]{:S(2)}, u32[]{:S(2)}) collective-permute-start(f16[32,2048]{1,0:T(8,128)(2,1)S(1)} %get-tuple-element.15), channel_id=1, source_target_pairs={{0,1},{1,0},{2,3},{3,2},{4,5},{5,4},{6,7},{7,6},{8,9},{9,8},{10,11... | collective-permute-start | bytes 393224 | tf_op jit(solution)/shard_map/ppermute | solution.py:18
  99.1 3.2 %collective-permute-done.14 = f16[32,2048]{1,0:T(8,128)(2,1)S(1)} collective-permute-done((f16[32,2048]{1,0:T(8,128)(2,1)S(1)}, f16[32,2048]{1,0:T(8,128)(2,1)S(1)}, u32[]{:S(2)}, u32[]{:S(2)}) %collective-permute-start.14) | collective-permute-done | bytes 131104 | tf_op jit(solution)/shard_map/ppermute | solution.py:18
  102.6 17.7 %update.1 = bf16[4096,2048]{1,0:T(8,128)(2,1)} custom-call(bf16[256,4096]{1,0:T(8,128)(2,1)S(1)} %constant_dynamic-update-slice_fusion.8.full_ref, f32[96,4096]{1,0:T(8,128)S(1)} %maximum_convert_fusion.b_ref, bf16[256,2048]{1,0:T(8,128)(2,1)S(1)} %bitcast.53, bf16[288,2048]{1,0:T(8,128)(2,1)S(1)} %copy-done.4, bf16[4096,2048]{1,0:T(8,128)(2,1)S(1)} %bitcast.51), custom_call_target="tpu_custom_call" | custom-call | tf_op jit(solution)/shard_map/update/pallas_call | solution.py:189
  (66 shorter events, 5.9 us)
Async XLA Ops:
  3.6 11.7 %collective-permute-start.1 = (f32[32,128]{1,0:T(8,128)S(1)}, f32[32,128]{1,0:T(8,128)S(1)}, u32[]{:S(2)}, u32[]{:S(2)}) collective-permute-start(f32[32,128]{1,0:T(8,128)S(1)} %convolution_reduce_fusion.1), channel_id=1, source_target_pairs={{0,1},{1,0},{2,3},{3,2},{4,5},{5,4},{6,7},{7,6},{8,9},{9,8},{10,11... | collective-permute-start | bytes 49160 | tf_op jit(solution)/shard_map/ppermute | solution.py:18
  6.6 8.7 %copy-start.1 = (bf16[1,256,2048]{2,1,0:T(8,128)(2,1)S(1)}, bf16[1,256,2048]{2,1,0:T(8,128)(2,1)}, u32[]{:S(2)}) copy-start(bf16[1,256,2048]{2,1,0:T(8,128)(2,1)} %param.6) | copy-start | bytes 3145732
  15.6 1.6 %collective-permute-start.2 = (f32[32,2048]{1,0:T(8,128)S(1)}, f32[32,2048]{1,0:T(8,128)S(1)}, u32[]{:S(2)}, u32[]{:S(2)}) collective-permute-start(f32[32,2048]{1,0:T(8,128)S(1)} %multiply_subtract_fusion), channel_id=1, source_target_pairs={{0,2},{2,0},{4,6},{6,4},{8,10},{10,8},{12,14},{14,12},{16,18},{18,... | collective-permute-start | bytes 786440 | tf_op jit(solution)/shard_map/ppermute | solution.py:18
  18.0 8.3 %collective-permute-start.3 = (f32[32,2048]{1,0:T(8,128)S(1)}, f32[32,2048]{1,0:T(8,128)S(1)}, u32[]{:S(2)}, u32[]{:S(2)}) collective-permute-start(f32[32,2048]{1,0:T(8,128)S(1)} %get-tuple-element.20), channel_id=1, source_target_pairs={{0,4},{2,6},{4,0},{6,2},{8,12},{10,14},{12,8},{14,10},{16,20},{18,... | collective-permute-start | bytes 786440 | tf_op jit(solution)/shard_map/ppermute | solution.py:18
  19.5 30.2 %collective-permute-start = (bf16[128,4096]{1,0:T(8,128)(2,1)}, bf16[128,4096]{1,0:T(8,128)(2,1)}, u32[]{:S(2)}, u32[]{:S(2)}) collective-permute-start(bf16[128,4096]{1,0:T(8,128)(2,1)} %bitcast), channel_id=1, source_target_pairs={{0,1},{1,0},{2,3},{3,2},{4,5},{5,4},{6,7},{7,6},{8,9},{9,8},{10,11... | collective-permute-start | bytes 3145736 | tf_op jit(solution)/shard_map/ppermute | solution.py:18
  27.1 7.7 %collective-permute-start.4 = (f32[32,2048]{1,0:T(8,128)S(1)}, f32[32,2048]{1,0:T(8,128)}, u32[]{:S(2)}, u32[]{:S(2)}) collective-permute-start(f32[32,2048]{1,0:T(8,128)S(1)} %get-tuple-element.22), channel_id=1, source_target_pairs={{0,8},{2,10},{4,12},{6,14},{8,0},{10,2},{12,4},{14,6},{16,24},{18,... | collective-permute-start | bytes 786440 | tf_op jit(solution)/shard_map/ppermute | solution.py:18
  37.8 7.9 %collective-permute-start.5 = (f32[96,96]{1,0:T(8,128)S(1)}, f32[96,96]{1,0:T(8,128)S(1)}, u32[]{:S(2)}, u32[]{:S(2)}) collective-permute-start(f32[96,96]{1,0:T(8,128)S(1)} %fusion.21), channel_id=1, source_target_pairs={{0,1},{1,0},{2,3},{3,2},{4,5},{5,4},{6,7},{7,6},{8,9},{9,8},{10,11... | collective-permute-start | bytes 110600 | tf_op jit(solution)/shard_map/ppermute | solution.py:18
  49.7 15.7 %copy-start.3 = (bf16[288,2048]{1,0:T(8,128)(2,1)}, bf16[288,2048]{1,0:T(8,128)(2,1)S(1)}, u32[]{:S(2)}) copy-start(bf16[288,2048]{1,0:T(8,128)(2,1)S(1)} %get-tuple-element.6.o_ref) | copy-start | bytes 3538948
  51.5 5.8 %copy-start = (bf16[1,4096,2048]{2,1,0:T(8,128)(2,1)S(1)}, bf16[1,4096,2048]{2,1,0:T(8,128)(2,1)}, u32[]{:S(2)}) copy-start(bf16[1,4096,2048]{2,1,0:T(8,128)(2,1)} %param.5) | copy-start | bytes 50331652
  66.3 12.9 %copy-start.5 = (f32[32,4096]{1,0:T(8,128)}, f32[32,4096]{1,0:T(8,128)S(1)}, u32[]{:S(2)}) copy-start(f32[32,4096]{1,0:T(8,128)S(1)} %get-tuple-element.17) | copy-start | bytes 1572868
  66.4 5.0 %collective-permute-start.6 = (f16[32,2048]{1,0:T(8,128)(2,1)S(1)}, f16[32,2048]{1,0:T(8,128)(2,1)S(1)}, u32[]{:S(2)}, u32[]{:S(2)}) collective-permute-start(f16[32,2048]{1,0:T(8,128)(2,1)S(1)} %dynamic-slice_convert_fusion.2), channel_id=1, source_target_pairs={{0,1},{1,0},{2,3},{3,2},{4,5},{5,4},{6,7},{7,6},{8,9},{9,8},{10,11... | collective-permute-start | bytes 393224 | tf_op jit(solution)/shard_map/ppermute | solution.py:18
  67.0 11.9 %copy-start.7 = (f32[32,4096]{1,0:T(8,128)S(1)}, f32[32,4096]{1,0:T(8,128)}, u32[]{:S(2)}) copy-start(f32[32,4096]{1,0:T(8,128)} %get-tuple-element.16) | copy-start | bytes 1572868
  71.4 3.2 %collective-permute-start.7 = (f32[32,2048]{1,0:T(8,128)S(1)}, f32[32,2048]{1,0:T(8,128)S(1)}, u32[]{:S(2)}, u32[]{:S(2)}) collective-permute-start(f32[32,2048]{1,0:T(8,128)S(1)} %convert_add_fusion.1), channel_id=1, source_target_pairs={{0,2},{2,0},{4,6},{6,4},{8,10},{10,8},{12,14},{14,12},{16,18},{18,... | collective-permute-start | bytes 786440 | tf_op jit(solution)/shard_map/ppermute | solution.py:18
  72.5 6.4 %collective-permute-start.9 = (f16[32,2048]{1,0:T(8,128)(2,1)S(1)}, f16[32,2048]{1,0:T(8,128)(2,1)S(1)}, u32[]{:S(2)}, u32[]{:S(2)}) collective-permute-start(f16[32,2048]{1,0:T(8,128)(2,1)S(1)} %dynamic-slice_convert_fusion.1), channel_id=1, source_target_pairs={{0,1},{1,0},{2,3},{3,2},{4,5},{5,4},{6,7},{7,6},{8,9},{9,8},{10,11... | collective-permute-start | bytes 393224 | tf_op jit(solution)/shard_map/ppermute | solution.py:18
  73.1 18.6 %collective-permute-start.12 = (f16[32,2048]{1,0:T(8,128)(2,1)S(1)}, f16[32,2048]{1,0:T(8,128)(2,1)S(1)}, u32[]{:S(2)}, u32[]{:S(2)}) collective-permute-start(f16[32,2048]{1,0:T(8,128)(2,1)S(1)} %dynamic-slice_convert_fusion), channel_id=1, source_target_pairs={{0,1},{1,0},{2,3},{3,2},{4,5},{5,4},{6,7},{7,6},{8,9},{9,8},{10,11... | collective-permute-start | bytes 393224 | tf_op jit(solution)/shard_map/ppermute | solution.py:18
  74.8 19.2 %collective-permute-start.8 = (f16[32,2048]{1,0:T(8,128)(2,1)S(1)}, f16[32,2048]{1,0:T(8,128)(2,1)S(1)}, u32[]{:S(2)}, u32[]{:S(2)}) collective-permute-start(f16[32,2048]{1,0:T(8,128)(2,1)S(1)} %get-tuple-element.11), channel_id=1, source_target_pairs={{0,1},{1,0},{2,3},{3,2},{4,5},{5,4},{6,7},{7,6},{8,9},{9,8},{10,11... | collective-permute-start | bytes 393224 | tf_op jit(solution)/shard_map/ppermute | solution.py:18
  79.2 23.3 %slice-start = ((s8[16777216]{0:T(1024)(128)(4,1)}), s8[4194304]{0:T(1024)(128)(4,1)S(1)}, s32[]{:S(2)}) async-start(s8[16777216]{0:T(1024)(128)(4,1)} %bitcast.49), calls=%async_computation | async-start | bytes 8388608
  79.3 12.5 %copy-start.6 = (f32[32,4096]{1,0:T(8,128)S(1)}, f32[32,4096]{1,0:T(8,128)}, u32[]{:S(2)}) copy-start(f32[32,4096]{1,0:T(8,128)} %copy-done.5) | copy-start | bytes 1572868
  79.3 23.3 %slice-start.1 = ((s8[16777216]{0:T(1024)(128)(4,1)}), s8[4194304]{0:T(1024)(128)(4,1)S(1)}, s32[]{:S(2)}) async-start(s8[16777216]{0:T(1024)(128)(4,1)} %bitcast.49), calls=%async_computation.1 | async-start | bytes 8388608
  79.3 23.3 %slice-start.2 = ((s8[16777216]{0:T(1024)(128)(4,1)}), s8[4194304]{0:T(1024)(128)(4,1)S(1)}, s32[]{:S(2)}) async-start(s8[16777216]{0:T(1024)(128)(4,1)} %bitcast.49), calls=%async_computation.2 | async-start | bytes 8388608
  79.3 23.3 %slice-start.3 = ((s8[16777216]{0:T(1024)(128)(4,1)}), s8[4194304]{0:T(1024)(128)(4,1)S(1)}, s32[]{:S(2)}) async-start(s8[16777216]{0:T(1024)(128)(4,1)} %bitcast.49), calls=%async_computation.3 | async-start | bytes 8388608
  79.3 11.9 %collective-permute-start.10 = (f16[32,2048]{1,0:T(8,128)(2,1)S(1)}, f16[32,2048]{1,0:T(8,128)(2,1)S(1)}, u32[]{:S(2)}, u32[]{:S(2)}) collective-permute-start(f16[32,2048]{1,0:T(8,128)(2,1)S(1)} %get-tuple-element.29), channel_id=1, source_target_pairs={{0,4},{2,6},{4,0},{6,2},{8,12},{10,14},{12,8},{14,10},{16,20},{18,... | collective-permute-start | bytes 393224 | tf_op jit(solution)/shard_map/ppermute | solution.py:18
  91.3 7.7 %collective-permute-start.11 = (f16[32,2048]{1,0:T(8,128)(2,1)S(1)}, f16[32,2048]{1,0:T(8,128)(2,1)S(1)}, u32[]{:S(2)}, u32[]{:S(2)}) collective-permute-start(f16[32,2048]{1,0:T(8,128)(2,1)S(1)} %get-tuple-element.13), channel_id=1, source_target_pairs={{0,1},{1,0},{2,3},{3,2},{4,5},{5,4},{6,7},{7,6},{8,9},{9,8},{10,11... | collective-permute-start | bytes 393224 | tf_op jit(solution)/shard_map/ppermute | solution.py:18
  92.1 10.4 %copy-start.2 = (bf16[1,256,2048]{2,1,0:T(8,128)(2,1)S(1)}, bf16[1,256,2048]{2,1,0:T(8,128)(2,1)}, u32[]{:S(2)}) copy-start(bf16[1,256,2048]{2,1,0:T(8,128)(2,1)} %param.6) | copy-start | bytes 3145732
  92.1 10.4 %copy-start.4 = (bf16[288,2048]{1,0:T(8,128)(2,1)S(1)}, bf16[288,2048]{1,0:T(8,128)(2,1)}, u32[]{:S(2)}) copy-start(bf16[288,2048]{1,0:T(8,128)(2,1)} %copy-done.3) | copy-start | bytes 3538948
  92.1 5.0 %collective-permute-start.13 = (f16[32,2048]{1,0:T(8,128)(2,1)S(1)}, f16[32,2048]{1,0:T(8,128)(2,1)S(1)}, u32[]{:S(2)}, u32[]{:S(2)}) collective-permute-start(f16[32,2048]{1,0:T(8,128)(2,1)S(1)} %get-tuple-element.31), channel_id=1, source_target_pairs={{0,8},{2,10},{4,12},{6,14},{8,0},{10,2},{12,4},{14,6},{16,24},{18,... | collective-permute-start | bytes 393224 | tf_op jit(solution)/shard_map/ppermute | solution.py:18
  97.3 5.0 %collective-permute-start.14 = (f16[32,2048]{1,0:T(8,128)(2,1)S(1)}, f16[32,2048]{1,0:T(8,128)(2,1)S(1)}, u32[]{:S(2)}, u32[]{:S(2)}) collective-permute-start(f16[32,2048]{1,0:T(8,128)(2,1)S(1)} %get-tuple-element.15), channel_id=1, source_target_pairs={{0,1},{1,0},{2,3},{3,2},{4,5},{5,4},{6,7},{7,6},{8,9},{9,8},{10,11... | collective-permute-start | bytes 393224 | tf_op jit(solution)/shard_map/ppermute | solution.py:18
